TPU v7x, 128 devices: a whole 4x4x4 slice. The times are simulated.
128 devices in a mesh: gx: 8 (over z_lo, x), gy: 16 (over y, z_hi, core).
Axes of the slice: x: 4, y: 4, z: 4 (z_hi: 2, z_lo: 2; z = z_hi * 2 + z_lo), core: 2. Of those that a mesh axis runs over, the one named last changes fastest.
Arguments:
- e_forward: float32 [3, 128, 512, 512], P(None, 'gx', 'gy'), may hold values from -6 to 6
- h_forward: float32 [3, 128, 512, 512], P(None, 'gx', 'gy'), may hold values from -6 to 6
- e_adjoint: float32 [3, 128, 512, 512], P(None, 'gx', 'gy'), may hold values from -6 to 6
- h_adjoint: float32 [3, 128, 512, 512], P(None, 'gx', 'gy'), may hold values from -6 to 6
- inv_eps: float32 [128, 512, 512], P('gx', 'gy'), may hold values from 0.08 to 1
- source: float32 [128, 512, 512], P('gx', 'gy'), may hold values from -6 to 6
- adj_source: float32 [128, 512, 512], P('gx', 'gy'), may hold values from -6 to 6
- design_mask: int32 [8, 16, 128], P('gx', 'gy'), may hold values from 0 to 1, as said below
- param_map: int32 [8, 16, 128], P('gx', 'gy'), may hold values from 0 to 8191, as said below
- step_index: int32 [1], replicated, may hold values from 0 to 4095
Outputs:
- design_grad: float32 [8192, 2048], P(('gx', 'gy'))
- e_forward_out: float32 [3, 128, 512, 512], P(None, 'gx', 'gy')
- e_adjoint_out: float32 [3, 128, 512, 512], P(None, 'gx', 'gy')
Inputs may be any that keep to these rules, and one draw needn't show every extreme that they name: `design_mask`: exactly 8192 blocks are 1; the number of 1s of one device varies from device to device, and some device has all its 128 blocks at 1. `param_map`: over the blocks with design_mask 1 the values are distinct and use every one of 0..8191; parameter p is owned by device p // 64 of gx+gy; a device's design blocks go to at most 1 parameters of any one owner, a bound that some device reaches; the values of other blocks mean nothing.
All inputs are finite; a program needn't handle non-finite values.
Results may differ from a plain program's by a relative error of at most 0.00013.
Values sent between devices are 32-bit elements; how exact they have to be, the bound alone decides.
No kernel may reach another device: no remote copies, remote signals or barrier semaphores. Data moves between devices by JAX's collectives and lax.ppermute only.
A program may use at most 256 MiB of HBM per device.

v0:
```python
import functools
import math

import jax
import jax.numpy as jnp
from jax import lax
from jax.experimental import pallas as pl
from jax.experimental.pallas import tpu as pltpu
from jax.sharding import PartitionSpec as P

BZ = 4
STEPS = 2
DT = 0.5
PERIOD = 20
RATE = 2.0 * math.pi / 20.0
CX, CY, NZ = 16, 32, 512
RING = 40
F32 = jnp.float32
VMEM_BYTES = (64 << 20) - (128 << 10)
TOUCH_BYTES, EDGE_BYTES, MAIN_BYTES, PACK_BYTES = 24 << 20, 24 << 20, 24 << 20, 32 << 20

UP, DOWN = 14, 10


def cycled(value, axis, by):
    devices = lax.axis_size(axis)
    return lax.ppermute(value, axis, [(i, (i + by) % devices) for i in range(devices)])


def rows_iota(shape):
    return lax.broadcasted_iota(jnp.int32, shape, 0)


def lanes_iota(shape):
    return lax.broadcasted_iota(jnp.int32, shape, 1)


def plus_y(f):
    return pltpu.roll(f, f.shape[0] - 1, 0) - f


def minus_y(f):
    return f - pltpu.roll(f, 1, 0)


def plus_z(f):
    return jnp.where(lanes_iota(f.shape) == NZ - 1, 0.0, pltpu.roll(f, NZ - 1, 1)) - f


def minus_z(f):
    return f - jnp.where(lanes_iota(f.shape) == 0, 0.0, pltpu.roll(f, 1, 1))


def magnetic(e, e_next, h, row_dt):
    ahead_y = -e[1] if e_next is None else e_next[1] - e[1]
    ahead_z = -e[2] if e_next is None else e_next[2] - e[2]
    return (
        h[0] - row_dt * (plus_y(e[2]) - plus_z(e[1])),
        h[1] - row_dt * (plus_z(e[0]) - ahead_z),
        h[2] - row_dt * (ahead_y - plus_y(e[0])),
    )


def electric(e, h, h_prev, coef, drive):
    back_y = h[1] if h_prev is None else h[1] - h_prev[1]
    back_z = h[2] if h_prev is None else h[2] - h_prev[2]
    return (
        e[0] + coef * (minus_y(h[2]) - minus_z(h[1])),
        e[1] + coef * (minus_z(h[0]) - back_z),
        e[2] + coef * (back_y - minus_y(h[0]) - drive),
    )


def amplitude(step_index, ticks, rows):
    tick = lax.rem(step_index[0] + (PERIOD + ticks), PERIOD)
    tile = jnp.sin(RATE * jnp.full((8, 128), tick, jnp.int32).astype(F32))
    return jnp.concatenate([jnp.concatenate([tile] * (NZ // 128), axis=1)] * (rows // 8), axis=0)


def dot_three(a, b):
    return a[0] * b[0] + a[1] * b[1] + a[2] * b[2]


def plus_x(f):
    return jnp.where(rows_iota(f.shape) == f.shape[0] - 1, 0.0, pltpu.roll(f, f.shape[0] - 1, 0)) - f


def minus_x(f):
    return f - jnp.where(rows_iota(f.shape) == 0, 0.0, pltpu.roll(f, 1, 0))


def has_rows():
    place = lax.axis_index("gy")
    return place < lax.axis_size("gy") - 1, place > 0


def row_steps():
    _, has_above = has_rows()
    rows = rows_iota((8, NZ))
    tile = jnp.where((rows >= 6) & jnp.logical_not(has_above), 0.0, DT)
    return jnp.concatenate([jnp.full((CY, NZ), DT, F32), tile], axis=0)


def ring_steps():
    _, has_above = has_rows()
    tile = jnp.where((rows_iota((8, NZ)) == 7) & has_above, DT, 0.0)
    return jnp.concatenate([jnp.full((CY, NZ), DT, F32), tile], axis=0)


class Ghosts:
    def __init__(self, above, below, x):
        has_below, has_above = has_rows()
        self.refs = above, below
        self.flags = jnp.where(has_above, 1.0, 0.0).astype(F32), jnp.where(has_below, 1.0, 0.0).astype(F32)
        self.x = x

    def up(self, k, x=None):
        return self.refs[0][k, pl.ds(self.x if x is None else x, 1), :] * self.flags[0]

    def down(self, k, x=None):
        return self.refs[1][k, pl.ds(self.x if x is None else x, 1), :] * self.flags[1]

    def tile(self, rows):
        at = rows_iota((8, NZ))
        tile = jnp.zeros((8, NZ), F32)
        for row, value in rows.items():
            tile = jnp.where(at == row, value, tile)
        return tile

    def e_before(self, run):
        return (
            self.tile({0: self.down(4 * run)}),
            jnp.zeros((8, NZ), F32),
            self.tile({0: self.down(4 * run + 1)}),
        )

    def e_middle(self, run):
        return (
            self.tile({0: self.down(4 * run + 2), 7: self.up(6 * run)}),
            self.tile({7: self.up(6 * run + 1)}),
            self.tile({0: self.down(4 * run + 3), 7: self.up(6 * run + 2)}),
        )

    def h_before(self, run):
        return tuple(self.tile({7: self.up(6 * run + 3 + c)}) for c in range(3))

    def coef(self):
        return DT * self.tile({0: self.down(8), 7: self.up(12)})


def ring(own, tile):
    return jnp.concatenate([own, tile], axis=0)


def rings(own, tiles):
    return tuple(ring(own[c], tiles[c]) for c in range(3))


def rows_up(amp, e_refs, h_refs, inv, drives, out):
    coef = DT * inv[:, 7, :]
    singles = []
    for run in range(2):
        e, e_in = ([e_refs[run][c, :, r, :] for c in range(3)] for r in (7, 6))
        h, h_in = ([h_refs[run][c, :, r, :] for c in range(3)] for r in (7, 6))
        hx_in = h_in[0] - DT * ((e[2] - e_in[2]) - plus_z(e_in[1]))
        hz_in = h_in[2] - DT * (plus_x(e_in[1]) - (e[0] - e_in[0]))
        out[6 * run] = e[0] - coef * hz_in
        out[6 * run + 1] = e[1]
        out[6 * run + 2] = e[2] + coef * (hx_in - amp[run] * drives[run][:, 7, :])
        out[6 * run + 3] = h[0] + DT * (e[2] + plus_z(e[1]))
        out[6 * run + 4] = h[1] - DT * (plus_z(e[0]) - plus_x(e[2]))
        out[6 * run + 5] = h[2] - DT * (plus_x(e[1]) + e[0])
        singles += [e[2], e_in[1]]
    out[12] = inv[:, 7, :]
    rows = rows_iota((CX, NZ))
    held = singles[0]
    for k in range(1, 4):
        held = jnp.where(rows == k, pltpu.roll(singles[k], k, 0), held)
    out[13] = held


def rows_down(amp, e_refs, h_refs, inv, drives, out):
    coef = DT * inv[:, 0, :]
    singles, others = [], []
    for run in range(2):
        e, e_in = ([e_refs[run][c, :, r, :] for c in range(3)] for r in (0, 1))
        h = [h_refs[run][c, :, 0, :] for c in range(3)]
        hx = h[0] - DT * ((e_in[2] - e[2]) - plus_z(e[1]))
        hy = h[1] - DT * (plus_z(e[0]) - plus_x(e[2]))
        hz = h[2] - DT * (plus_x(e[1]) - (e_in[0] - e[0]))
        out[4 * run] = e[0]
        out[4 * run + 1] = e[2]
        out[4 * run + 2] = e[0] + coef * (hz - minus_z(hy))
        out[4 * run + 3] = e[2] + coef * (minus_x(hy) - hx - amp[run] * drives[run][:, 0, :])
        singles.append(e[1])
        others.append(hy)
    out[8] = inv[:, 0, :]
    rows = rows_iota((CX, NZ))
    held = singles[0]
    for k, (value, by) in enumerate([(singles[1], 1), (others[0], 3), (others[1], 4)], 1):
        held = jnp.where(rows == k, pltpu.roll(value, by, 0), held)
    out[9] = held


def pack_kernel(step_index, e_f, h_f, e_a, h_a, inv, src, adj, far_up, far_down, *scratch):
    sources = (e_f, h_f, e_a, h_a, inv, src, adj)
    places, (up, down, sems, out_sems) = scratch[:7], scratch[7:]
    stores = [pltpu.make_async_copy(up, far_up, out_sems.at[0]), pltpu.make_async_copy(down, far_down, out_sems.at[1])]

    def load(a, side):
        at = pl.ds(24 if side == 0 else 0, 8)
        source = sources[a].at[:, :, at] if a < 4 else sources[a].at[:, at]
        return pltpu.make_async_copy(source, places[a].at[side], sems.at[a, side])

    for side in range(2):
        for a in range(7):
            load(a, side).start()
    amp = [amplitude(step_index, ticks, CX) for ticks in (1, -1)]
    for side, (rows_of, out) in enumerate([(rows_up, up), (rows_down, down)]):
        for a in range(7):
            load(a, side).wait()
        ef, hf, ea, ha, coef, drive_f, drive_a = (place.at[side] for place in places)
        rows_of(amp, (ef, ea), (hf, ha), coef, (drive_f, drive_a), out)
        stores[side].start()
    for copy in stores:
        copy.wait()


def pack_rows(step_index, arrays):
    hbm = pl.BlockSpec(memory_space=pl.ANY)
    shapes = [(UP, CX, NZ), (DOWN, CX, NZ)]
    return pl.pallas_call(
        pack_kernel,
        in_specs=[pl.BlockSpec(memory_space=pltpu.SMEM)] + [hbm] * 7,
        out_specs=[hbm] * 2,
        out_shape=[jax.ShapeDtypeStruct(s, F32) for s in shapes],
        scratch_shapes=[pltpu.VMEM((2, 3, CX, 8, NZ), F32)] * 4
        + [pltpu.VMEM((2, CX, 8, NZ), F32)] * 3
        + [pltpu.VMEM(s, F32) for s in shapes]
        + [pltpu.SemaphoreType.DMA((7, 2)), pltpu.SemaphoreType.DMA((2,))],
        compiler_params=pltpu.CompilerParams(vmem_limit_bytes=VMEM_BYTES),
        cost_estimate=pl.CostEstimate(flops=4 * 10**9, bytes_accessed=0, transcendentals=0),
        name="pack_rows",
    )(step_index, *arrays)


def touch_kernel(*refs):
    refs[-1][...] = refs[4][0, :8, :128]


def touch(arrays):
    whole = pl.BlockSpec(memory_space=pltpu.VMEM)
    return pl.pallas_call(
        touch_kernel,
        in_specs=[whole] * 7,
        out_specs=whole,
        out_shape=jax.ShapeDtypeStruct((8, 128), F32),
        compiler_params=pltpu.CompilerParams(vmem_limit_bytes=TOUCH_BYTES),
        cost_estimate=pl.CostEstimate(flops=6 * 10**9, bytes_accessed=0, transcendentals=0),
        name="touch",
    )(*arrays)


def write_layers(out, values):
    rows = rows_iota((8, NZ))
    for k, value in enumerate(values):
        out[pl.ds(CY * k, CY), :] = value[:CY]
    for k in range(0, 9, 2):
        tile = pltpu.roll(values[k][CY:], 2, 0)
        if k < 8:
            tile = jnp.where(rows < 4, tile, pltpu.roll(values[k + 1][CY:], 6, 0))
        out[pl.ds(9 * CY + 4 * k, 8), :] = tile


def read_layer(ref, k):
    tile = ref[pl.ds(9 * CY + 8 * (k // 2), 8), :]
    return ring(ref[pl.ds(CY * k, CY), :], pltpu.roll(tile, 2 if k % 2 else 6, 0))


def call_edges(kernel, name, step_index, arrays, messages, shapes):
    whole = pl.BlockSpec(memory_space=pltpu.VMEM)

    def body(step_index, *refs):
        sides = []
        for side in range(2):
            at = pl.ds(side * (CX - 2), 2)
            sides += [refs[a].at[:, at] if a < 4 else refs[a].at[at] for a in range(7)]
        kernel(step_index, *sides, *refs[7:9], *refs[10:])

    return pl.pallas_call(
        body,
        in_specs=[pl.BlockSpec(memory_space=pltpu.SMEM)] + [whole] * (7 + len(messages)),
        out_specs=[whole] * len(shapes),
        out_shape=[jax.ShapeDtypeStruct(s, F32) for s in shapes],
        compiler_params=pltpu.CompilerParams(vmem_limit_bytes=EDGE_BYTES),
        cost_estimate=pl.CostEstimate(flops=3 * 10**9, bytes_accessed=0, transcendentals=0),
        name=name,
    )(step_index, *arrays, *messages)


def edge_kernel(step_index, e_f0, h_f0, e_a0, h_a0, inv0, src0, adj0, e_f1, h_f1, e_a1, h_a1, inv1, src1, adj1, above, below, out_prev, out_next, keep):
    row_dt = ring_steps()
    ghosts = {x: Ghosts(above, below, x) for x in (0, 1, CX - 2, CX - 1)}
    still = jnp.zeros((8, NZ), F32)
    amp = [amplitude(step_index, ticks, CY) for ticks in (1, -1)]

    def before(ref, at, run, x):
        return rings([ref[c, at] for c in range(3)], ghosts[x].e_before(run))

    def middle(ref, at, run, x):
        return rings([ref[c, at] for c in range(3)], ghosts[x].e_middle(run))

    def magnet(ref, at, run, x):
        return rings([ref[c, at] for c in range(3)], ghosts[x].h_before(run))

    coef_first = ring(DT * inv0[0], ghosts[0].coef())
    coef_last = ring(DT * inv1[1], ghosts[CX - 1].coef())
    to_prev, to_next = [None] * 9, [None] * 9
    to_prev[8] = coef_first
    to_next[8] = coef_last
    for run, (e0, h0, s0, e1, h1, s1) in enumerate(
        [(e_f0, h_f0, src0, e_f1, h_f1, src1), (e_a0, h_a0, adj0, e_a1, h_a1, adj1)]
    ):
        near = ghosts[0]
        h = magnetic(before(e0, 0, run, 0), before(e0, 1, run, 1), magnet(h0, 0, run, 0), row_dt)
        drive = ring(amp[run] * s0[0], still)
        new = electric(middle(e0, 0, run, 0), h, None, coef_first, drive)
        sides_y = {0: near.down(9, run), 6: near.up(13, 2 * run + 1), 7: near.up(6 * run + 1)}
        sides_z = {0: near.down(4 * run + 1), 7: near.up(13, 2 * run)}
        to_prev[4 * run] = ring(e0[1, 0], near.tile(sides_y))
        to_prev[4 * run + 1] = ring(e0[2, 0], near.tile(sides_z))
        to_prev[4 * run + 2] = new[1]
        to_prev[4 * run + 3] = new[2]
        keep[4 * run] = new[0][:CY]
        e, back = before(e1, 1, run, CX - 1), before(e1, 0, run, CX - 2)
        h = magnetic(e, None, magnet(h1, 1, run, CX - 1), row_dt)
        h_back = magnetic(back, e, magnet(h1, 0, run, CX - 2), row_dt)
        drive = ring(amp[run] * s1[1], still)
        new = electric(middle(e1, 1, run, CX - 1), h, h_back, coef_last, drive)
        later = magnetic(new, None, h, row_dt)
        beyond = ghosts[CX - 1].down(9, 2 + run)
        to_next[4 * run] = jnp.where(rows_iota((RING, NZ)) == CY, beyond, h[1])
        to_next[4 * run + 1] = h[2]
        to_next[4 * run + 2] = later[1]
        to_next[4 * run + 3] = later[2]
        for c in range(3):
            keep[4 * run + 1 + c] = new[c][:CY]
    write_layers(out_prev, to_prev)
    write_layers(out_next, to_next)


def solve_edges(step_index, arrays, above, below, touched):
    shapes = [(9 * CY + 40, NZ), (9 * CY + 40, NZ), (8, CY, NZ)]
    return call_edges(edge_kernel, "solve_edges", step_index, arrays, [above, below, touched], shapes)


CHUNK = 2
DRAIN = 4


def zplus(tile):
    moved = pltpu.roll(tile, NZ - 1, 1)
    last = jnp.where(lanes_iota((8, 128)) == 127, 0.0, moved[:, NZ - 128 :])
    return jnp.concatenate([moved[:, : NZ - 128], last], axis=1) - tile


def zminus(tile):
    moved = pltpu.roll(tile, 1, 1)
    first = jnp.where(lanes_iota((8, 128)) == 0, 0.0, moved[:, :128])
    return tile - jnp.concatenate([first, moved[:, 128:]], axis=1)


def magnetic_tiles(tiles, e, e_next, h, row_dts, put, closed):
    end = rows_iota((8, NZ)) == 7
    firsts = {c: pltpu.roll(e(c, 0), 7, 0) for c in (0, 2)}
    here = firsts
    for t in range(tiles):
        if t == tiles - 1:
            after = {c: jnp.zeros((8, NZ), F32) for c in (0, 2)} if closed else firsts
        else:
            after = {c: pltpu.roll(e(c, t + 1), 7, 0) for c in (0, 2)}
        ex, ey, ez = (e(c, t) for c in range(3))
        put(0, t, h(0, t) - row_dts[t] * ((jnp.where(end, after[2], here[2]) - ez) - zplus(ey)))
        put(1, t, h(1, t) - row_dts[t] * (zplus(ex) - (e_next(2, t) - ez)))
        put(2, t, h(2, t) - row_dts[t] * ((e_next(1, t) - ey) - (jnp.where(end, after[0], here[0]) - ex)))
        here = after


def electric_tile(e, h, h_prev, coef, drive, t, rolled):
    start = rows_iota((8, NZ)) == 0
    hx, hy, hz = (h(c, t) for c in range(3))
    moved = {0: pltpu.roll(hx, 1, 0), 2: pltpu.roll(hz, 1, 0)}
    new_x = e(0, t) + coef * ((hz - jnp.where(start, rolled[2], moved[2])) - zminus(hy))
    new_y = e(1, t) + coef * (zminus(hx) - (hz - h_prev(2, t)))
    curl = (hy - h_prev(1, t)) - (hx - jnp.where(start, rolled[0], moved[0]))
    new_z = e(2, t) + coef * (curl if drive is None else curl - drive)
    return (new_x, new_y, new_z), moved


def sweep(step_index, places, store, mid_h, mid_e, late_h, tiles, at_rows, ghosts, put_last):
    v_ef, v_hf, v_ea, v_ha, v_inv, v_src, v_adj = places
    own = [t for t in range(tiles) if at_rows[t] is not None]
    closed = len(own) == tiles
    mid_h[...] = jnp.zeros_like(mid_h)
    late_h[...] = jnp.zeros_like(late_h)
    ghost_dt = None if closed else ring_steps()[CY:]
    row_dts = [DT if t in own else ghost_dt for t in range(tiles)]
    amp = [[amplitude(step_index, ticks, 8) for ticks in pair] for pair in ((1, 2), (-1, -2))]
    runs = ((v_ef, v_hf, v_src), (v_ea, v_ha, v_adj))
    nothing = {c: jnp.zeros((8, NZ), F32) for c in (0, 2)}

    def rows(t):
        return pl.ds(at_rows[t], 8)

    def ring_rows(t):
        return pl.ds(8 * t, 8)

    def one(step, carry):
        now, then = lax.rem(step, 2), lax.rem(step + 1, 2)

        @pl.when(step <= CX)
        def _():
            x = step - 1
            inside, x_next = step < CX, jnp.minimum(step, CX - 1)
            if not closed:
                here, there = ghosts(x), ghosts(jnp.minimum(step, CX - 1))
                coef_ghost = here.coef()
            for run, (e_ref, h_ref, s_ref) in enumerate(runs):
                beside = beside_next = beside_h = middle = None
                if not closed:
                    beside = here.e_before(run)
                    beside_next = [jnp.where(inside, v, 0.0) for v in there.e_before(run)]
                    beside_h = here.h_before(run)
                    middle = here.e_middle(run)

                def put_h(c, t, value):
                    mid_h[now, 3 * run + c, ring_rows(t), :] = value

                magnetic_tiles(
                    tiles,
                    lambda c, t: e_ref[c, x, rows(t), :] if t in own else beside[c],
                    lambda c, t: jnp.where(inside, e_ref[c, x_next, rows(t), :], 0.0) if t in own else beside_next[c],
                    lambda c, t: h_ref[c, x, rows(t), :] if t in own else beside_h[c],
                    row_dts,
                    put_h,
                    closed,
                )
                rolled = nothing
                if not closed:
                    end = ring_rows(tiles - 1)
                    rolled = {c: pltpu.roll(mid_h[now, 3 * run + c, end, :], 1, 0) for c in (0, 2)}
                for t in range(tiles):
                    if t in own:
                        coef, drive = DT * v_inv[x, rows(t), :], amp[run][0] * s_ref[x, rows(t), :]
                    else:
                        coef, drive = coef_ghost, None
                    new, rolled = electric_tile(
                        lambda c, t: e_ref[c, x, rows(t), :] if t in own else middle[c],
                        lambda c, t: mid_h[now, 3 * run + c, ring_rows(t), :],
                        lambda c, t: mid_h[then, 3 * run + c, ring_rows(t), :],
                        coef,
                        drive,
                        t,
                        rolled,
                    )
                    for c in range(3):
                        mid_e[now, 3 * run + c, ring_rows(t), :] = new[c]

        @pl.when(step > CX)
        def _():
            mid_e[now] = jnp.zeros((6, 8 * tiles, NZ), F32)

        @pl.when(step > 1)
        def _():
            x = step - 2
            rolled = [nothing, nothing]
            for run in range(2):

                def put_late(c, t, value):
                    late_h[now, 3 * run + c, ring_rows(t), :] = value

                magnetic_tiles(
                    tiles,
                    lambda c, t: mid_e[then, 3 * run + c, ring_rows(t), :],
                    lambda c, t: mid_e[now, 3 * run + c, ring_rows(t), :],
                    lambda c, t: mid_h[then, 3 * run + c, ring_rows(t), :],
                    row_dts,
                    put_late,
                    closed,
                )
            for t in range(tiles):
                if t not in own:
                    rolled = [
                        {c: pltpu.roll(late_h[now, 3 * run + c, ring_rows(t), :], 1, 0) for c in (0, 2)}
                        for run in range(2)
                    ]
                    continue
                coef = DT * v_inv[x, rows(t), :]
                new = [None, None]
                for run, (e_ref, _, s_ref) in enumerate(runs):
                    new[run], rolled[run] = electric_tile(
                        lambda c, t: mid_e[then, 3 * run + c, ring_rows(t), :],
                        lambda c, t: late_h[now, 3 * run + c, ring_rows(t), :],
                        lambda c, t: late_h[then, 3 * run + c, ring_rows(t), :],
                        coef,
                        amp[run][1] * s_ref[x, rows(t), :],
                        t,
                        rolled[run],
                    )
                first = [[mid_e[then, 3 * run + c, ring_rows(t), :] for c in range(3)] for run in range(2)]
                put_last(x, t, new, DT * (dot_three(*first) + dot_three(*new)))

        @pl.when((step > 2) & (step % DRAIN == 1))
        def _():
            for a in range(2):
                store(a, step // DRAIN - 1).start()

        return carry

    lax.fori_loop(1, CX + 2, one, 0)
    for part in range(CX // DRAIN):
        for a in range(2):
            store(a, part).wait()


def main_kernel(
    step_index, e_f, h_f, e_a, h_a, inv, src, adj, above, below, out_f, out_a, grad,
    last_f, last_a, mid_h, mid_e, late_h, store_sem,
):
    def store(a, part):
        at = pl.ds(part * DRAIN, DRAIN)
        return pltpu.make_async_copy((last_f, last_a)[a].at[:, at], (out_f, out_a)[a].at[:, at], store_sem.at[a, part])

    def put_last(x, t, new, product):
        for c in range(3):
            last_f[c, x, pl.ds(8 * t - 8, 8), :] = new[0][c]
            last_a[c, x, pl.ds(8 * t - 8, 8), :] = new[1][c]
        grad[x, pl.ds(8 * t - 8, 8), :] = product

    sweep(
        step_index, (e_f, h_f, e_a, h_a, inv, src, adj), store, mid_h, mid_e, late_h, 5, [None, 0, 8, 16, 24],
        lambda x: Ghosts(above, below, x), put_last,
    )


def solve_main(step_index, arrays, above, below):
    free, whole = pl.BlockSpec(memory_space=pl.ANY), pl.BlockSpec(memory_space=pltpu.VMEM)
    field, cells = (3, CX, CY, NZ), (CX, CY, NZ)
    return pl.pallas_call(
        main_kernel,
        in_specs=[pl.BlockSpec(memory_space=pltpu.SMEM)] + [whole] * 9,
        out_specs=[free, free, whole],
        out_shape=[jax.ShapeDtypeStruct(s, F32) for s in (field, field, cells)],
        scratch_shapes=[pltpu.VMEM(field, F32)] * 2
        + [pltpu.VMEM((2, 6, RING, NZ), F32)] * 3
        + [pltpu.SemaphoreType.DMA((2, CX // DRAIN))],
        compiler_params=pltpu.CompilerParams(vmem_limit_bytes=MAIN_BYTES),
        cost_estimate=pl.CostEstimate(flops=14 * 10**9, bytes_accessed=0, transcendentals=0),
        name="solve_main",
    )(step_index, *arrays, above, below)


def split(value):
    high = value.astype(jnp.bfloat16)
    return high, (value - high.astype(F32)).astype(jnp.bfloat16)


def exact_dot(a, b, dims):
    high, low = split(b)
    a = a.astype(jnp.bfloat16)
    return lax.dot_general(a, high, dims, preferred_element_type=F32) + lax.dot_general(
        a, low, dims, preferred_element_type=F32
    )


def correct_prev(run, from_prev, own, row_dt, present):
    e0y, e0z, e1y, e1z = (own[4 * run + k] for k in range(4))
    coef, ghost_coef = own[8], jnp.where(present, from_prev[8], 0.0)
    h1y, h1z, h2y, h2z = (from_prev[4 * run + k] for k in range(4))
    d_h1y, d_h1z = DT * e0z, -DT * e0y
    h1y = jnp.where(present, h1y + d_h1y, 0.0)
    h1z = jnp.where(present, h1z + d_h1z, 0.0)
    d_e1y, d_e1z = coef * h1z, -coef * h1y
    g_e1x = ghost_coef * (minus_y(d_h1z) - minus_z(d_h1y))
    g_e1y, g_e1z = -ghost_coef * d_h1z, ghost_coef * d_h1y
    h2y = jnp.where(present, h2y + d_h1y - DT * (plus_z(g_e1x) - (e1z + d_e1z - g_e1z)), 0.0)
    h2z = jnp.where(present, h2z + d_h1z - DT * ((e1y + d_e1y - g_e1y) - plus_y(g_e1x)), 0.0)
    d_h2x = -row_dt * (plus_y(d_e1z) - plus_z(d_e1y))
    d_h2y, d_h2z = -row_dt * d_e1z, row_dt * d_e1y
    first = (None, d_e1y, d_e1z)
    last = (
        coef * (minus_y(d_h2z) - minus_z(d_h2y)),
        d_e1y + coef * (minus_z(d_h2x) - d_h2z + h2z),
        d_e1z + coef * (d_h2y - h2y - minus_y(d_h2x)),
    )
    return first, last, d_h2y, d_h2z


def correct_next(run, from_next, own, row_dt, present):
    e0y, e0z, e1y, e1z = (jnp.where(present, from_next[4 * run + k], 0.0) for k in range(4))
    coef, ghost_coef = own[8], jnp.where(present, from_next[8], 0.0)
    h1y, h1z = own[4 * run], own[4 * run + 1]
    d_h1y, d_h1z = DT * e0z, -DT * e0y
    d_e1x = coef * (minus_y(d_h1z) - minus_z(d_h1y))
    d_e1y, d_e1z = -coef * d_h1z, coef * d_h1y
    e1y = e1y + ghost_coef * (h1z + d_h1z)
    e1z = e1z - ghost_coef * (h1y + d_h1y)
    d_h2x = -row_dt * (plus_y(d_e1z) - plus_z(d_e1y))
    d_h2y = d_h1y - row_dt * (plus_z(d_e1x) - (e1z - d_e1z))
    d_h2z = d_h1z - row_dt * ((e1y - d_e1y) - plus_y(d_e1x))
    b_h2y, b_h2z = row_dt * d_e1z, -row_dt * d_e1y
    first = (d_e1x, d_e1y, d_e1z)
    last = (
        d_e1x + coef * (minus_y(d_h2z) - minus_z(d_h2y)),
        d_e1y + coef * (minus_z(d_h2x) - d_h2z + b_h2z),
        d_e1z + coef * (d_h2y - b_h2y - minus_y(d_h2x)),
    )
    return first, last, b_h2y, b_h2z


def put_cells(chosen, values, rows_out, q):
    devices = rows_out.shape[0]
    cells = exact_dot(chosen[...], values.reshape(4 * CY, NZ), (((1,), (1,)), ((), ())))
    for part in range(BZ):
        at = part * CX * CY + q * 4 * CY
        rows_out[:, 0, at : at + 4 * CY] = cells[part * devices : (part + 1) * devices]


def inner_kernel(mask, param, grad, rows_out, chosen):
    devices = rows_out.shape[0]
    lanes = lanes_iota((devices, NZ))
    blocks = lax.broadcasted_iota(jnp.int32, (NZ // BZ, NZ), 0)
    spread = (blocks == lanes_iota((NZ // BZ, NZ)) // BZ).astype(jnp.bfloat16)
    owned = NZ // BZ // 2
    owner = jnp.where(mask[0] == 1, param[0] // owned, -1).astype(F32)
    slot = (param[0] & (owned - 1)).astype(F32)
    numbers = jnp.concatenate([owner, slot, jnp.zeros((14, NZ // BZ), F32)], axis=0)
    numbers = jnp.dot(numbers.astype(jnp.bfloat16), spread, preferred_element_type=F32)
    mine = numbers[0:1, :] == rows_iota((devices, NZ)).astype(F32)
    for part in range(BZ):
        chosen[pl.ds(part * devices, devices), :] = jnp.where(mine & (lanes % BZ == part), 1.0, 0.0).astype(jnp.bfloat16)
    found = jnp.sum(jnp.where(mine & (lanes % BZ == 0), numbers[1:2, :] + 1.0, 0.0), axis=1, keepdims=True) - 1.0
    rows_out[:, 0, BZ * CX * CY :] = jnp.broadcast_to(found, (devices, 128))

    for q in (1, 2):
        put_cells(chosen, grad[pl.ds(4 * q, 4)], rows_out, q)


def pack_inner(mask, param, grad, devices):
    whole = pl.BlockSpec(memory_space=pltpu.VMEM)
    return pl.pallas_call(
        inner_kernel,
        in_specs=[whole] * 3,
        out_specs=[whole] * 2,
        out_shape=[
            jax.ShapeDtypeStruct((devices, 1, BZ * CX * CY + 128), F32),
            jax.ShapeDtypeStruct((BZ * devices, NZ), jnp.bfloat16),
        ],
        compiler_params=pltpu.CompilerParams(vmem_limit_bytes=PACK_BYTES),
        cost_estimate=pl.CostEstimate(flops=2 * 10**9, bytes_accessed=0, transcendentals=0),
        name="pack_inner",
    )(mask, param, grad)


def correct_kernel(
    chosen, *refs
):
    far, refs = refs[:5], refs[5:]
    far_inv, far_grad, old_f, old_a, _, out_f, out_a, far_rows, *refs = refs
    near, refs = refs[:5], refs[5:]
    (
    v_inv, work, v_f, v_a, rows_out,
    message_sem, inv_sem, grad_sem, field_sem, store_sem, rows_sem,
    ) = refs
    ref_from_prev, ref_to_prev, keep, ref_from_next, ref_to_next = near
    place = lax.axis_index("gx")
    has_prev, has_next = place > 0, place < lax.axis_size("gx") - 1
    row_dt = row_steps()
    messages = [pltpu.make_async_copy(a, b, message_sem.at[k]) for k, (a, b) in enumerate(zip(far, near))]
    grads = [
        pltpu.make_async_copy(far_grad.at[pl.ds(4 * q, 4)], work.at[pl.ds(4 * q, 4)], grad_sem.at[q]) for q in (0, 3)
    ]
    ends, stores = [], []
    for side in range(2):
        at = pl.ds(side * (CX - 2), 2)
        ends.append(
            [
                pltpu.make_async_copy(far_inv.at[at], v_inv.at[side], inv_sem.at[side]),
                pltpu.make_async_copy(old_f.at[:, at], v_f.at[side], field_sem.at[0, side]),
                pltpu.make_async_copy(old_a.at[:, at], v_a.at[side], field_sem.at[1, side]),
            ]
        )
        stores.append(
            [
                pltpu.make_async_copy(v_f.at[side], out_f.at[:, at], store_sem.at[0, side]),
                pltpu.make_async_copy(v_a.at[side], out_a.at[:, at], store_sem.at[1, side]),
            ]
        )
    for copy in [*messages[:3], *ends[0], grads[0], *messages[3:], *ends[1], grads[1]]:
        copy.start()

    def finish(side, edge_at, inner_at, firsts, lasts, d_inner, inner_coef, base_first):
        total_f, total_a, inner_f, inner_a = [], [], [], []
        fields_f, fields_a = v_f.at[side], v_a.at[side]
        before = jnp.zeros((CY, NZ), F32)
        for c in range(3):
            before = before + fields_f[c, inner_at] * fields_a[c, inner_at]
        for run, (ref, total, inner) in enumerate([(fields_f, total_f, inner_f), (fields_a, total_a, inner_a)]):
            for c in range(3):
                total.append(ref[c, edge_at] + lasts[run][c][:CY])
                ref[c, edge_at] = total[c]
                add = d_inner[run][c]
                inner.append(ref[c, inner_at] if add is None else ref[c, inner_at] + inner_coef * add[:CY])
                ref[c, inner_at] = inner[c]
        e1 = [
            [base_first[run][c] if firsts[run][c] is None else base_first[run][c] + firsts[run][c][:CY] for c in range(3)]
            for run in range(2)
        ]
        edge_grad = DT * (dot_three(e1[0], e1[1]) + dot_three(total_f, total_a))
        inner_change = DT * (dot_three(inner_f, inner_a) - before)
        return edge_grad, inner_change

    def first_edge():
        firsts, lasts, d_inner, base = [], [], [], []
        from_prev, to_prev = ([read_layer(ref, k) for k in range(9)] for ref in (ref_from_prev, ref_to_prev))
        for run in range(2):
            first, last, d_h2y, d_h2z = correct_prev(run, from_prev, to_prev, row_dt, has_prev)
            firsts.append(first)
            lasts.append(last)
            d_inner.append((None, d_h2z, -d_h2y))
            base.append((keep[4 * run], to_prev[4 * run + 2][:CY], to_prev[4 * run + 3][:CY]))
        edge, inner = finish(0, 0, 1, firsts, lasts, d_inner, DT * v_inv[0, 1], base)
        work[0] = edge
        work[1] = work[1] + inner

    def last_edge():
        firsts, lasts, d_inner, base = [], [], [], []
        from_next = [read_layer(ref_from_next, k) for k in range(9)]
        to_next = {k: read_layer(ref_to_next, k) for k in (0, 1, 4, 5, 8)}
        for run in range(2):
            first, last, b_h2y, b_h2z = correct_next(run, from_next, to_next, row_dt, has_next)
            firsts.append(first)
            lasts.append(last)
            d_inner.append((minus_y(b_h2z) - minus_z(b_h2y), -b_h2z, b_h2y))
            base.append(tuple(keep[4 * run + 1 + c] for c in range(3)))
        edge, inner = finish(1, 1, 0, firsts, lasts, d_inner, DT * v_inv[1, 0], base)
        work[CX - 1] = edge
        work[CX - 2] = work[CX - 2] + inner

    row_copies = []

    def pack(q):
        put_cells(chosen, work[pl.ds(4 * q, 4)], rows_out, q)
        for part in range(BZ):
            columns = pl.ds(part * CX * CY + q * 4 * CY, 4 * CY)
            row_copies.append(
                pltpu.make_async_copy(rows_out.at[:, :, columns], far_rows.at[:, :, columns], rows_sem.at[q, part])
            )
            row_copies[-1].start()

    for copy in [*messages[:3], *ends[0], grads[0]]:
        copy.wait()
    first_edge()
    for copy in stores[0]:
        copy.start()
    pack(0)
    for copy in [*messages[3:], *ends[1], grads[1]]:
        copy.wait()
    last_edge()
    for copy in stores[1]:
        copy.start()
    pack(3)
    for copy in [*stores[0], *stores[1], *row_copies]:
        copy.wait()


def correct_and_pack(chosen, messages, inv, grad, fields_f, fields_a, rows):
    free, whole = pl.BlockSpec(memory_space=pl.ANY), pl.BlockSpec(memory_space=pltpu.VMEM)
    vmem = lambda shape: pltpu.VMEM(shape, F32)
    return pl.pallas_call(
        correct_kernel,
        in_specs=[whole] + [free] * 10,
        out_specs=[free] * 3,
        out_shape=[
            jax.ShapeDtypeStruct((3, CX, CY, NZ), F32),
            jax.ShapeDtypeStruct((3, CX, CY, NZ), F32),
            jax.ShapeDtypeStruct(rows.shape, F32),
        ],
        scratch_shapes=[vmem(m.shape) for m in messages]
        + [vmem((2, 2, CY, NZ)), vmem((CX, CY, NZ))]
        + [vmem((2, 3, 2, CY, NZ))] * 2
        + [vmem(rows.shape)]
        + [pltpu.SemaphoreType.DMA(s) for s in ((5,), (2,), (4,), (2, 2), (2, 2), (4, BZ))],
        input_output_aliases={8: 0, 9: 1, 10: 2},
        compiler_params=pltpu.CompilerParams(vmem_limit_bytes=PACK_BYTES),
        cost_estimate=pl.CostEstimate(flops=6 * 10**9, bytes_accessed=0, transcendentals=0),
        name="correct_and_pack",
    )(chosen, *messages, inv, grad, fields_f, fields_a, rows)


def place_kernel(got, out):
    devices = got.shape[0]
    owned = out.shape[0]
    cells = BZ * CX * CY
    numbers = got[:, 0, cells:]
    wanted = (numbers == lanes_iota((devices, 128)).astype(F32)).astype(F32)
    placing = jnp.transpose(wanted)[:owned]
    order_from = rows_iota((4 * 128, 4 * 128))
    order_to = lanes_iota((4 * 128, 4 * 128))
    order = (order_from == (order_to % BZ) * 128 + order_to // BZ).astype(jnp.bfloat16)
    dims = (((1,), (0,)), ((), ()))
    for q in range(4):
        parts = [got[:, 0, part * CX * CY + q * 128 : part * CX * CY + (q + 1) * 128] for part in range(BZ)]
        rows = exact_dot(placing, jnp.concatenate(parts, axis=1), dims)
        high, low = split(rows)
        out[:, q * 512 : (q + 1) * 512] = lax.dot_general(
            high, order, dims, preferred_element_type=F32
        ) + lax.dot_general(low, order, dims, preferred_element_type=F32)


def place_rows(got, owned):
    return pl.pallas_call(
        place_kernel,
        out_shape=jax.ShapeDtypeStruct((owned, BZ * CX * CY), F32),
        compiler_params=pltpu.CompilerParams(vmem_limit_bytes=32 << 20),
        cost_estimate=pl.CostEstimate(flops=2 * 10**9, bytes_accessed=0, transcendentals=0),
        name="place_rows",
    )(got)


def body(e_forward, h_forward, e_adjoint, h_adjoint, inv_eps, source, adj_source, design_mask, param_map, step_index):
    arrays = (e_forward, h_forward, e_adjoint, h_adjoint, inv_eps, source, adj_source)
    devices = lax.axis_size("gx") * lax.axis_size("gy")
    blocks = NZ // BZ
    owned = blocks // 2
    up, down = pack_rows(step_index, arrays)
    above, below = cycled(up, "gy", 1), cycled(down, "gy", -1)
    touched = touch(arrays)
    to_prev, to_next, keep = solve_edges(step_index, arrays, above, below, touched)
    from_next, from_prev = cycled(to_prev, "gx", -1), cycled(to_next, "gx", 1)
    fields_f, fields_a, grad = solve_main(step_index, arrays, above, below)
    messages = (from_prev, to_prev, keep, from_next, to_next)
    rows, chosen = pack_inner(design_mask, param_map, grad, devices)
    fields_f, fields_a, rows = correct_and_pack(chosen, messages, inv_eps, grad, fields_f, fields_a, rows)
    got = lax.all_to_all(rows, ("gx", "gy"), split_axis=0, concat_axis=0, tiled=True)
    return place_rows(got, owned), fields_f, fields_a


def solution(mesh):
    field, cells = P(None, "gx", "gy", None), P("gx", "gy", None)
    in_specs = (field, field, field, field, cells, cells, cells, cells, cells, P())
    out_specs = (P(("gx", "gy"), None), field, field)
    return jax.shard_map(body, mesh=mesh, in_specs=in_specs, out_specs=out_specs, check_vma=False)
```

profile of v0, /device:TPU:1, one launch (start us, length us, event | category | flops | bytes accessed | tf_op | source)
XLA Modules:
  0.0 78.7 jit_solution(13122396617412354662)
XLA Ops:
  1.3 4.4 %pack_rows.1 = (f32[14,16,512]{2,1,0:T(8,128)}, f32[10,16,512]{2,1,0:T(8,128)}) custom-call(s32[1]{0:T(128)S(6)} %copy.19.step_index, f32[3,16,32,512]{3,2,1,0:T(8,128)} %refs_0_.3, f32[3,16,32,512]{3,2,1,0:T(8,128)} %refs_1_.3, f32[3,16,32,512]{3,2,1,0:T(8,128)} %refs_2_.3, f32[3,16,32,512]{3,2,1,0:T(8,128)} %refs_3_.3, f32[16,32,512]{2,1,0:T(8,128)} %refs_5_.5, ...), custom_call_target="tpu_custom_call" | custom-call | flops 4000000000 | tf_op jit(solution)/shard_map/pack_rows/pallas_call | solution.py:232
  5.6 1.5 %collective-permute-start.1 = (f32[10,16,512]{2,1,0:T(8,128)}, f32[10,16,512]{2,1,0:T(8,128)S(1)}, u32[]{:S(2)}, u32[]{:S(2)}) collective-permute-start(f32[10,16,512]{2,1,0:T(8,128)} %get-tuple-element.17), channel_id=1, source_target_pairs={{0,15},{1,0},{2,1},{3,2},{4,3},{5,4},{6,5},{7,6},{8,7},{9,8},{10,9... | collective-permute-start | bytes 983048 | tf_op jit(solution)/shard_map/ppermute | solution.py:27
  7.1 3.6 %collective-permute-start = (f32[14,16,512]{2,1,0:T(8,128)}, f32[14,16,512]{2,1,0:T(8,128)S(1)}, u32[]{:S(2)}, u32[]{:S(2)}) collective-permute-start(f32[14,16,512]{2,1,0:T(8,128)} %get-tuple-element.16), channel_id=1, source_target_pairs={{0,1},{1,2},{2,3},{3,4},{4,5},{5,6},{6,7},{7,8},{8,9},{9,10},{10,1... | collective-permute-start | bytes 1376264 | tf_op jit(solution)/shard_map/ppermute | solution.py:27
  10.8 0.0 copy-start
  10.8 1.9 %copy-done = f32[3,16,32,512]{3,2,1,0:T(8,128)S(1)} copy-done((f32[3,16,32,512]{3,2,1,0:T(8,128)S(1)}, f32[3,16,32,512]{3,2,1,0:T(8,128)}, u32[]{:S(2)}) %copy-start) | copy-done | bytes 3145752
  12.7 0.0 copy-start.1
  12.7 1.9 %copy-done.1 = f32[3,16,32,512]{3,2,1,0:T(8,128)S(1)} copy-done((f32[3,16,32,512]{3,2,1,0:T(8,128)S(1)}, f32[3,16,32,512]{3,2,1,0:T(8,128)}, u32[]{:S(2)}) %copy-start.1) | copy-done | bytes 3145752
  14.6 0.0 copy-start.2
  14.6 1.9 %copy-done.2 = f32[3,16,32,512]{3,2,1,0:T(8,128)S(1)} copy-done((f32[3,16,32,512]{3,2,1,0:T(8,128)S(1)}, f32[3,16,32,512]{3,2,1,0:T(8,128)}, u32[]{:S(2)}) %copy-start.2) | copy-done | bytes 3145752
  16.5 0.0 copy-start.3
  16.5 1.9 %copy-done.3 = f32[3,16,32,512]{3,2,1,0:T(8,128)S(1)} copy-done((f32[3,16,32,512]{3,2,1,0:T(8,128)S(1)}, f32[3,16,32,512]{3,2,1,0:T(8,128)}, u32[]{:S(2)}) %copy-start.3) | copy-done | bytes 3145752
  18.3 0.0 copy-start.4
  18.3 1.2 %copy-done.4 = f32[16,32,512]{2,1,0:T(8,128)S(1)} copy-done((f32[16,32,512]{2,1,0:T(8,128)S(1)}, f32[16,32,512]{2,1,0:T(8,128)}, u32[]{:S(2)}) %copy-start.4) | copy-done | bytes 1048600
  19.6 0.0 copy-start.5
  19.6 1.2 %copy-done.5 = f32[16,32,512]{2,1,0:T(8,128)S(1)} copy-done((f32[16,32,512]{2,1,0:T(8,128)S(1)}, f32[16,32,512]{2,1,0:T(8,128)}, u32[]{:S(2)}) %copy-start.5) | copy-done | bytes 1048600
  20.8 1.2 %copy-done.6 = f32[16,32,512]{2,1,0:T(8,128)S(1)} copy-done((f32[16,32,512]{2,1,0:T(8,128)S(1)}, f32[16,32,512]{2,1,0:T(8,128)}, u32[]{:S(2)}) %copy-start.6) | copy-done | bytes 1048600
  22.0 0.0 collective-permute-done.1.below.refs_8_
  22.0 0.0 collective-permute-done.above.refs_7_
  22.0 0.9 %solve_edges.1 = (f32[328,512]{1,0:T(8,128)S(1)}, f32[328,512]{1,0:T(8,128)S(1)}, f32[8,32,512]{2,1,0:T(8,128)S(1)}) custom-call(s32[1]{0:T(128)S(6)} %copy.19.step_index, f32[3,16,32,512]{3,2,1,0:T(8,128)S(1)} %copy-done, f32[3,16,32,512]{3,2,1,0:T(8,128)S(1)} %copy-done.1, f32[3,16,32,512]{3,2,1,0:T(8,128)S(1)} %copy-done.2, ...), custom_call_target="tpu_custom_call" | custom-call | flops 3000000000 | tf_op jit(solution)/shard_map/solve_edges/pallas_call | solution.py:290
  22.9 1.3 %collective-permute-start.2 = (f32[328,512]{1,0:T(8,128)S(1)}, f32[328,512]{1,0:T(8,128)S(1)}, u32[]{:S(2)}, u32[]{:S(2)}) collective-permute-start(f32[328,512]{1,0:T(8,128)S(1)} %get-tuple-element.20.refs_4_), channel_id=1, source_target_pairs={{0,16},{16,32},{32,48},{48,64},{64,80},{80,96},{96,112},{112,0},{1... | collective-permute-start | bytes 2015240 | tf_op jit(solution)/shard_map/ppermute | solution.py:27
  24.2 2.4 %collective-permute-start.3 = (f32[328,512]{1,0:T(8,128)S(1)}, f32[328,512]{1,0:T(8,128)S(1)}, u32[]{:S(2)}, u32[]{:S(2)}) collective-permute-start(f32[328,512]{1,0:T(8,128)S(1)} %get-tuple-element.21.refs_1_), channel_id=1, source_target_pairs={{0,112},{16,0},{32,16},{48,32},{64,48},{80,64},{96,80},{112,96},{1... | collective-permute-start | bytes 2015240 | tf_op jit(solution)/shard_map/ppermute | solution.py:27
  26.6 13.3 %solve_main.1 = (f32[3,16,32,512]{3,2,1,0:T(8,128)}, f32[3,16,32,512]{3,2,1,0:T(8,128)}, f32[16,32,512]{2,1,0:T(8,128)S(1)}) custom-call(s32[1]{0:T(128)S(6)} %copy.19.step_index, f32[3,16,32,512]{3,2,1,0:T(8,128)S(1)} %copy-done, f32[3,16,32,512]{3,2,1,0:T(8,128)S(1)} %copy-done.1, f32[3,16,32,512]{3,2,1,0:T(8,128)S(1)} %copy-done.2, ...), custom_call_target="tpu_custom_call" | custom-call | flops 14000000000 | tf_op jit(solution)/shard_map/solve_main/pallas_call | solution.py:549
  39.9 0.0 copy-done.8
  39.9 0.0 copy-done.9
  39.9 0.0 copy-start.7
  39.9 1.0 %pack_inner.1 = (f32[128,1,2176]{2,1,0:T(1,128)S(1)}, bf16[512,512]{1,0:T(8,128)(2,1)S(1)}) custom-call(s32[1,1,128]{2,1,0:T(1,128)S(1)} %copy-done.8, s32[1,1,128]{2,1,0:T(1,128)S(1)} %copy-done.9, f32[16,32,512]{2,1,0:T(8,128)S(1)} %get-tuple-element.18.grad.refs_6_), custom_call_target="tpu_custom_call" | custom-call | flops 2000000000 | tf_op jit(solution)/shard_map/pack_inner/pallas_call | solution.py:651
  41.0 0.0 collective-permute-done.2.refs_0_
  41.0 0.0 collective-permute-done.3.refs_3_
  41.0 0.1 copy-done.7
  41.1 4.9 %correct_and_pack.1 = (f32[3,16,32,512]{3,2,1,0:T(8,128)}, f32[3,16,32,512]{3,2,1,0:T(8,128)}, f32[128,1,2176]{2,1,0:T(1,128)S(1)}) custom-call(bf16[512,512]{1,0:T(8,128)(2,1)S(1)} %get-tuple-element.19.chosen, f32[328,512]{1,0:T(8,128)S(1)} %collective-permute-done.2.refs_0_, ...), custom_call_target="tpu_custom_call", output_to_operand_aliasing={{0}: (8, {}), {1}: (9, {}), {2}: (10, {})} | custom-call | flops 6000000000 | tf_op jit(solution)/shard_map/correct_and_pack/pallas_call | solution.py:780
  46.0 30.3 %all_to_all.5.got = f32[128,1,2176]{2,1,0:T(1,128)S(1)} all-to-all(f32[128,1,2176]{2,1,0:T(1,128)S(1)} %get-tuple-element.26), channel_id=1, replica_groups=mesh['gx'=8,'gy'=16] {'gx','gy'}, dimensions={0} | all-to-all | bytes 2228224 | tf_op jit(solution)/shard_map/all_to_all | solution.py:845
  76.3 2.4 %place_rows.1 = f32[64,2048]{1,0:T(8,128)} custom-call(f32[128,1,2176]{2,1,0:T(1,128)S(1)} %all_to_all.5.got), custom_call_target="tpu_custom_call" | custom-call | flops 2000000000 | tf_op jit(solution)/shard_map/place_rows/pallas_call | solution.py:822
  (4 shorter events, 0.0 us)
Async XLA Ops:
  5.6 16.4 %collective-permute-start.1 = (f32[10,16,512]{2,1,0:T(8,128)}, f32[10,16,512]{2,1,0:T(8,128)S(1)}, u32[]{:S(2)}, u32[]{:S(2)}) collective-permute-start(f32[10,16,512]{2,1,0:T(8,128)} %get-tuple-element.17), channel_id=1, source_target_pairs={{0,15},{1,0},{2,1},{3,2},{4,3},{5,4},{6,5},{7,6},{8,7},{9,8},{10,9... | collective-permute-start | bytes 983048 | tf_op jit(solution)/shard_map/ppermute | solution.py:27
  7.1 14.9 %collective-permute-start = (f32[14,16,512]{2,1,0:T(8,128)}, f32[14,16,512]{2,1,0:T(8,128)S(1)}, u32[]{:S(2)}, u32[]{:S(2)}) collective-permute-start(f32[14,16,512]{2,1,0:T(8,128)} %get-tuple-element.16), channel_id=1, source_target_pairs={{0,1},{1,2},{2,3},{3,4},{4,5},{5,6},{6,7},{7,8},{8,9},{9,10},{10,1... | collective-permute-start | bytes 1376264 | tf_op jit(solution)/shard_map/ppermute | solution.py:27
  10.8 1.9 %copy-start = (f32[3,16,32,512]{3,2,1,0:T(8,128)S(1)}, f32[3,16,32,512]{3,2,1,0:T(8,128)}, u32[]{:S(2)}) copy-start(f32[3,16,32,512]{3,2,1,0:T(8,128)} %refs_0_.3) | copy-start | bytes 9437188
  12.7 1.9 %copy-start.1 = (f32[3,16,32,512]{3,2,1,0:T(8,128)S(1)}, f32[3,16,32,512]{3,2,1,0:T(8,128)}, u32[]{:S(2)}) copy-start(f32[3,16,32,512]{3,2,1,0:T(8,128)} %refs_1_.3) | copy-start | bytes 9437188
  14.6 1.9 %copy-start.2 = (f32[3,16,32,512]{3,2,1,0:T(8,128)S(1)}, f32[3,16,32,512]{3,2,1,0:T(8,128)}, u32[]{:S(2)}) copy-start(f32[3,16,32,512]{3,2,1,0:T(8,128)} %refs_2_.3) | copy-start | bytes 9437188
  16.5 1.9 %copy-start.3 = (f32[3,16,32,512]{3,2,1,0:T(8,128)S(1)}, f32[3,16,32,512]{3,2,1,0:T(8,128)}, u32[]{:S(2)}) copy-start(f32[3,16,32,512]{3,2,1,0:T(8,128)} %refs_3_.3) | copy-start | bytes 9437188
  18.3 1.2 %copy-start.4 = (f32[16,32,512]{2,1,0:T(8,128)S(1)}, f32[16,32,512]{2,1,0:T(8,128)}, u32[]{:S(2)}) copy-start(f32[16,32,512]{2,1,0:T(8,128)} %refs_5_.4) | copy-start | bytes 3145732
  19.6 1.2 %copy-start.5 = (f32[16,32,512]{2,1,0:T(8,128)S(1)}, f32[16,32,512]{2,1,0:T(8,128)}, u32[]{:S(2)}) copy-start(f32[16,32,512]{2,1,0:T(8,128)} %refs_6_.3) | copy-start | bytes 3145732
  20.8 1.2 %copy-start.6 = (f32[16,32,512]{2,1,0:T(8,128)S(1)}, f32[16,32,512]{2,1,0:T(8,128)}, u32[]{:S(2)}) copy-start(f32[16,32,512]{2,1,0:T(8,128)} %refs_5_.5) | copy-start | bytes 3145732
  22.9 18.0 %collective-permute-start.2 = (f32[328,512]{1,0:T(8,128)S(1)}, f32[328,512]{1,0:T(8,128)S(1)}, u32[]{:S(2)}, u32[]{:S(2)}) collective-permute-start(f32[328,512]{1,0:T(8,128)S(1)} %get-tuple-element.20.refs_4_), channel_id=1, source_target_pairs={{0,16},{16,32},{32,48},{48,64},{64,80},{80,96},{96,112},{112,0},{1... | collective-permute-start | bytes 2015240 | tf_op jit(solution)/shard_map/ppermute | solution.py:27
  24.2 15.7 %copy-start.8 = (s32[1,1,128]{2,1,0:T(1,128)S(1)}, s32[1,1,128]{2,1,0:T(1,128)}, u32[]{:S(2)}) copy-start(s32[1,1,128]{2,1,0:T(1,128)} %mask.1) | copy-start | bytes 1540
  24.2 15.7 %copy-start.9 = (s32[1,1,128]{2,1,0:T(1,128)S(1)}, s32[1,1,128]{2,1,0:T(1,128)}, u32[]{:S(2)}) copy-start(s32[1,1,128]{2,1,0:T(1,128)} %param.21) | copy-start | bytes 1540
  24.2 16.8 %collective-permute-start.3 = (f32[328,512]{1,0:T(8,128)S(1)}, f32[328,512]{1,0:T(8,128)S(1)}, u32[]{:S(2)}, u32[]{:S(2)}) collective-permute-start(f32[328,512]{1,0:T(8,128)S(1)} %get-tuple-element.21.refs_1_), channel_id=1, source_target_pairs={{0,112},{16,0},{32,16},{48,32},{64,48},{80,64},{96,80},{112,96},{1... | collective-permute-start | bytes 2015240 | tf_op jit(solution)/shard_map/ppermute | solution.py:27
  39.9 1.2 %copy-start.7 = (f32[16,32,512]{2,1,0:T(8,128)S(1)}, f32[16,32,512]{2,1,0:T(8,128)}, u32[]{:S(2)}) copy-start(f32[16,32,512]{2,1,0:T(8,128)} %refs_5_.5) | copy-start | bytes 3145732
where the time goes:
time: 79.2 us; the launch traced here: 78.7 us
  blocking collectives  30.3 us (38%)
  Pallas kernels  26.9 us (34%)
  local copies, waits for them, and re-layouts  11.4 us (14%)
  starting transfers between devices  8.78 us (11%)
  between operations  1.37 us (2%)
    all_to_all x1, blocking collectives, body(): lax.all_to_all(rows, ('gx', 'gy'), split_axis=0, concat_axis=0, tiled=True)  30.3 us
    pallas_call x1, Pallas kernels, solve_main(): pl.pallas_call(main_kernel, in_specs=[pl.BlockSpec(memory_space=pltpu.SME...  13.3 us
    unnamed x20, local copies, waits for them, and re-layouts  11.4 us
    ppermute x4, starting transfers between devices, cycled(): lax.ppermute(value, axis, [(i, (i + by) % devices) for i in range(devices)])  8.78 us
    pallas_call x1, Pallas kernels, correct_and_pack(): pl.pallas_call(correct_kernel, in_specs=[whole] + [free] * 10, out_specs=...  4.9 us
    pallas_call x1, Pallas kernels, pack_rows(): pl.pallas_call(pack_kernel, in_specs=[pl.BlockSpec(memory_space=pltpu.SME...  4.36 us
    pallas_call x1, Pallas kernels, place_rows(): pl.pallas_call(place_kernel, out_shape=jax.ShapeDtypeStruct((owned, BZ *...  2.42 us
  transfers between devices with their start and end apart: 4, of which 0 were waited for; matrix products, arithmetic and copies ran while one was open for 0% of the time, Pallas kernels for 18%

commit v1 on v0

--- a/solution.py
+++ b/solution.py
@@ -665,14 +665,14 @@
 def correct_kernel(
     chosen, *refs
 ):
-    far, refs = refs[:5], refs[5:]
+    (ref_to_prev, keep, ref_to_next), far, refs = refs[:3], refs[3:5], refs[5:]
     far_inv, far_grad, old_f, old_a, _, out_f, out_a, far_rows, *refs = refs
-    near, refs = refs[:5], refs[5:]
+    near, refs = refs[:2], refs[2:]
     (
     v_inv, work, v_f, v_a, rows_out,
     message_sem, inv_sem, grad_sem, field_sem, store_sem, rows_sem,
     ) = refs
-    ref_from_prev, ref_to_prev, keep, ref_from_next, ref_to_next = near
+    ref_from_prev, ref_from_next = near
     place = lax.axis_index("gx")
     has_prev, has_next = place > 0, place < lax.axis_size("gx") - 1
     row_dt = row_steps()
@@ -696,7 +696,7 @@
                 pltpu.make_async_copy(v_a.at[side], out_a.at[:, at], store_sem.at[1, side]),
             ]
         )
-    for copy in [*messages[:3], *ends[0], grads[0], *messages[3:], *ends[1], grads[1]]:
+    for copy in [*messages[:1], *ends[0], grads[0], *messages[1:], *ends[1], grads[1]]:
         copy.start()
 
     def finish(side, edge_at, inner_at, firsts, lasts, d_inner, inner_coef, base_first):
@@ -758,13 +758,13 @@
             )
             row_copies[-1].start()
 
-    for copy in [*messages[:3], *ends[0], grads[0]]:
+    for copy in [*messages[:1], *ends[0], grads[0]]:
         copy.wait()
     first_edge()
     for copy in stores[0]:
         copy.start()
     pack(0)
-    for copy in [*messages[3:], *ends[1], grads[1]]:
+    for copy in [*messages[1:], *ends[1], grads[1]]:
         copy.wait()
     last_edge()
     for copy in stores[1]:
@@ -779,18 +779,18 @@
     vmem = lambda shape: pltpu.VMEM(shape, F32)
     return pl.pallas_call(
         correct_kernel,
-        in_specs=[whole] + [free] * 10,
+        in_specs=[whole] * 4 + [free] * 7,
         out_specs=[free] * 3,
         out_shape=[
             jax.ShapeDtypeStruct((3, CX, CY, NZ), F32),
             jax.ShapeDtypeStruct((3, CX, CY, NZ), F32),
             jax.ShapeDtypeStruct(rows.shape, F32),
         ],
-        scratch_shapes=[vmem(m.shape) for m in messages]
+        scratch_shapes=[vmem(m.shape) for m in messages[3:]]
         + [vmem((2, 2, CY, NZ)), vmem((CX, CY, NZ))]
         + [vmem((2, 3, 2, CY, NZ))] * 2
         + [vmem(rows.shape)]
-        + [pltpu.SemaphoreType.DMA(s) for s in ((5,), (2,), (4,), (2, 2), (2, 2), (4, BZ))],
+        + [pltpu.SemaphoreType.DMA(s) for s in ((2,), (2,), (4,), (2, 2), (2, 2), (4, BZ))],
         input_output_aliases={8: 0, 9: 1, 10: 2},
         compiler_params=pltpu.CompilerParams(vmem_limit_bytes=PACK_BYTES),
         cost_estimate=pl.CostEstimate(flops=6 * 10**9, bytes_accessed=0, transcendentals=0),
@@ -839,7 +839,7 @@
     to_prev, to_next, keep = solve_edges(step_index, arrays, above, below, touched)
     from_next, from_prev = cycled(to_prev, "gx", -1), cycled(to_next, "gx", 1)
     fields_f, fields_a, grad = solve_main(step_index, arrays, above, below)
-    messages = (from_prev, to_prev, keep, from_next, to_next)
+    messages = (to_prev, keep, to_next, from_prev, from_next)
     rows, chosen = pack_inner(design_mask, param_map, grad, devices)
     fields_f, fields_a, rows = correct_and_pack(chosen, messages, inv_eps, grad, fields_f, fields_a, rows)
     got = lax.all_to_all(rows, ("gx", "gy"), split_axis=0, concat_axis=0, tiled=True)

time: 79.2 us -> 79 us (level)
  waiting for transfers between devices: 0.01 us -> 1.32 us
    ppermute x4, waiting for transfers between devices: 0.01 us -> 1.32 us  [cycled(): lax.ppermute(value, axis, [(i, (i + by) % devices) for i in range(devices)])]
  transfers between devices with their start and end apart: 4 -> 4, of which waited for: 0 -> 1; matrix products, arithmetic and copies ran while one was open for 0% -> 0% of each run, Pallas kernels for 18% -> 18%
where the time goes in v1:
time: 79 us; the launch traced here: 78.5 us
  blocking collectives  29.8 us (38%)
  Pallas kernels  26.6 us (34%)
  local copies, waits for them, and re-layouts  11.2 us (14%)
  starting transfers between devices  8.14 us (10%)
  between operations  1.36 us (2%)
  waiting for transfers between devices  1.32 us (2%)
    all_to_all x1, blocking collectives, body(): lax.all_to_all(rows, ('gx', 'gy'), split_axis=0, concat_axis=0, tiled=True)  29.8 us
    pallas_call x1, Pallas kernels, solve_main(): pl.pallas_call(main_kernel, in_specs=[pl.BlockSpec(memory_space=pltpu.SME...  13.3 us
    unnamed x20, local copies, waits for them, and re-layouts  11.2 us
    ppermute x4, starting transfers between devices, cycled(): lax.ppermute(value, axis, [(i, (i + by) % devices) for i in range(devices)])  8.14 us
    pallas_call x1, Pallas kernels, correct_and_pack(): pl.pallas_call(correct_kernel, in_specs=[whole] * 4 + [free] * 7, out_spe...  4.63 us
    pallas_call x1, Pallas kernels, pack_rows(): pl.pallas_call(pack_kernel, in_specs=[pl.BlockSpec(memory_space=pltpu.SME...  4.36 us
    pallas_call x1, Pallas kernels, place_rows(): pl.pallas_call(place_kernel, out_shape=jax.ShapeDtypeStruct((owned, BZ *...  2.42 us
  transfers between devices with their start and end apart: 4, of which 1 were waited for; matrix products, arithmetic and copies ran while one was open for 0% of the time, Pallas kernels for 18%

profile of v1, /device:TPU:1, one launch (start us, length us, event | category | flops | bytes accessed | tf_op | source)
XLA Modules:
  0.0 78.5 jit_solution(2189088187404563261)
XLA Ops:
  1.3 4.4 %pack_rows.1 = (f32[14,16,512]{2,1,0:T(8,128)}, f32[10,16,512]{2,1,0:T(8,128)}) custom-call(s32[1]{0:T(128)S(6)} %copy.19.step_index, f32[3,16,32,512]{3,2,1,0:T(8,128)} %refs_0_.3, f32[3,16,32,512]{3,2,1,0:T(8,128)} %refs_1_.3, f32[3,16,32,512]{3,2,1,0:T(8,128)} %refs_2_.3, f32[3,16,32,512]{3,2,1,0:T(8,128)} %refs_3_.3, f32[16,32,512]{2,1,0:T(8,128)} %refs_5_.5, ...), custom_call_target="tpu_custom_call" | custom-call | flops 4000000000 | tf_op jit(solution)/shard_map/pack_rows/pallas_call | solution.py:232
  5.6 1.5 %collective-permute-start.1 = (f32[10,16,512]{2,1,0:T(8,128)}, f32[10,16,512]{2,1,0:T(8,128)S(1)}, u32[]{:S(2)}, u32[]{:S(2)}) collective-permute-start(f32[10,16,512]{2,1,0:T(8,128)} %get-tuple-element.17), channel_id=1, source_target_pairs={{0,15},{1,0},{2,1},{3,2},{4,3},{5,4},{6,5},{7,6},{8,7},{9,8},{10,9... | collective-permute-start | bytes 983048 | tf_op jit(solution)/shard_map/ppermute | solution.py:27
  7.1 3.6 %collective-permute-start = (f32[14,16,512]{2,1,0:T(8,128)}, f32[14,16,512]{2,1,0:T(8,128)S(1)}, u32[]{:S(2)}, u32[]{:S(2)}) collective-permute-start(f32[14,16,512]{2,1,0:T(8,128)} %get-tuple-element.16), channel_id=1, source_target_pairs={{0,1},{1,2},{2,3},{3,4},{4,5},{5,6},{6,7},{7,8},{8,9},{9,10},{10,1... | collective-permute-start | bytes 1376264 | tf_op jit(solution)/shard_map/ppermute | solution.py:27
  10.8 0.0 copy-start
  10.8 1.9 %copy-done = f32[3,16,32,512]{3,2,1,0:T(8,128)S(1)} copy-done((f32[3,16,32,512]{3,2,1,0:T(8,128)S(1)}, f32[3,16,32,512]{3,2,1,0:T(8,128)}, u32[]{:S(2)}) %copy-start) | copy-done | bytes 3145752
  12.7 0.0 copy-start.1
  12.7 1.9 %copy-done.1 = f32[3,16,32,512]{3,2,1,0:T(8,128)S(1)} copy-done((f32[3,16,32,512]{3,2,1,0:T(8,128)S(1)}, f32[3,16,32,512]{3,2,1,0:T(8,128)}, u32[]{:S(2)}) %copy-start.1) | copy-done | bytes 3145752
  14.6 0.0 copy-start.2
  14.6 1.9 %copy-done.2 = f32[3,16,32,512]{3,2,1,0:T(8,128)S(1)} copy-done((f32[3,16,32,512]{3,2,1,0:T(8,128)S(1)}, f32[3,16,32,512]{3,2,1,0:T(8,128)}, u32[]{:S(2)}) %copy-start.2) | copy-done | bytes 3145752
  16.5 0.0 copy-start.3
  16.5 1.9 %copy-done.3 = f32[3,16,32,512]{3,2,1,0:T(8,128)S(1)} copy-done((f32[3,16,32,512]{3,2,1,0:T(8,128)S(1)}, f32[3,16,32,512]{3,2,1,0:T(8,128)}, u32[]{:S(2)}) %copy-start.3) | copy-done | bytes 3145752
  18.3 0.0 copy-start.4
  18.3 1.2 %copy-done.4 = f32[16,32,512]{2,1,0:T(8,128)S(1)} copy-done((f32[16,32,512]{2,1,0:T(8,128)S(1)}, f32[16,32,512]{2,1,0:T(8,128)}, u32[]{:S(2)}) %copy-start.4) | copy-done | bytes 1048600
  19.6 0.0 copy-start.5
  19.6 1.2 %copy-done.5 = f32[16,32,512]{2,1,0:T(8,128)S(1)} copy-done((f32[16,32,512]{2,1,0:T(8,128)S(1)}, f32[16,32,512]{2,1,0:T(8,128)}, u32[]{:S(2)}) %copy-start.5) | copy-done | bytes 1048600
  20.8 1.2 %copy-done.6 = f32[16,32,512]{2,1,0:T(8,128)S(1)} copy-done((f32[16,32,512]{2,1,0:T(8,128)S(1)}, f32[16,32,512]{2,1,0:T(8,128)}, u32[]{:S(2)}) %copy-start.6) | copy-done | bytes 1048600
  22.0 0.0 collective-permute-done.1.below.refs_8_
  22.0 0.0 collective-permute-done.above.refs_7_
  22.0 0.9 %solve_edges.1 = (f32[328,512]{1,0:T(8,128)S(1)}, f32[328,512]{1,0:T(8,128)S(1)}, f32[8,32,512]{2,1,0:T(8,128)S(1)}) custom-call(s32[1]{0:T(128)S(6)} %copy.19.step_index, f32[3,16,32,512]{3,2,1,0:T(8,128)S(1)} %copy-done, f32[3,16,32,512]{3,2,1,0:T(8,128)S(1)} %copy-done.1, f32[3,16,32,512]{3,2,1,0:T(8,128)S(1)} %copy-done.2, ...), custom_call_target="tpu_custom_call" | custom-call | flops 3000000000 | tf_op jit(solution)/shard_map/solve_edges/pallas_call | solution.py:290
  22.9 3.0 %collective-permute-start.3 = (f32[328,512]{1,0:T(8,128)S(1)}, f32[328,512]{1,0:T(8,128)S(1)}, u32[]{:S(2)}, u32[]{:S(2)}) collective-permute-start(f32[328,512]{1,0:T(8,128)S(1)} %get-tuple-element.20.refs_0_), channel_id=1, source_target_pairs={{0,112},{16,0},{32,16},{48,32},{64,48},{80,64},{96,80},{112,96},{1... | collective-permute-start | bytes 2015240 | tf_op jit(solution)/shard_map/ppermute | solution.py:27
  25.9 0.0 collective-permute-start.2
  25.9 13.3 %solve_main.1 = (f32[3,16,32,512]{3,2,1,0:T(8,128)}, f32[3,16,32,512]{3,2,1,0:T(8,128)}, f32[16,32,512]{2,1,0:T(8,128)S(1)}) custom-call(s32[1]{0:T(128)S(6)} %copy.19.step_index, f32[3,16,32,512]{3,2,1,0:T(8,128)S(1)} %copy-done, f32[3,16,32,512]{3,2,1,0:T(8,128)S(1)} %copy-done.1, f32[3,16,32,512]{3,2,1,0:T(8,128)S(1)} %copy-done.2, ...), custom_call_target="tpu_custom_call" | custom-call | flops 14000000000 | tf_op jit(solution)/shard_map/solve_main/pallas_call | solution.py:549
  39.2 0.0 copy-done.8
  39.2 0.0 copy-done.9
  39.2 0.0 copy-start.7
  39.3 1.0 %pack_inner.1 = (f32[128,1,2176]{2,1,0:T(1,128)S(1)}, bf16[512,512]{1,0:T(8,128)(2,1)S(1)}) custom-call(s32[1,1,128]{2,1,0:T(1,128)S(1)} %copy-done.8, s32[1,1,128]{2,1,0:T(1,128)S(1)} %copy-done.9, f32[16,32,512]{2,1,0:T(8,128)S(1)} %get-tuple-element.18.grad.refs_6_), custom_call_target="tpu_custom_call" | custom-call | flops 2000000000 | tf_op jit(solution)/shard_map/pack_inner/pallas_call | solution.py:651
  40.3 0.0 collective-permute-done.3.refs_4_
  40.3 1.3 %collective-permute-done.2.refs_3_ = f32[328,512]{1,0:T(8,128)S(1)} collective-permute-done((f32[328,512]{1,0:T(8,128)S(1)}, f32[328,512]{1,0:T(8,128)S(1)}, u32[]{:S(2)}, u32[]{:S(2)}) %collective-permute-start.2) | collective-permute-done | bytes 671776 | tf_op jit(solution)/shard_map/ppermute | solution.py:27
  41.6 0.0 copy-done.7
  41.6 4.6 %correct_and_pack.1 = (f32[3,16,32,512]{3,2,1,0:T(8,128)}, f32[3,16,32,512]{3,2,1,0:T(8,128)}, f32[128,1,2176]{2,1,0:T(1,128)S(1)}) custom-call(bf16[512,512]{1,0:T(8,128)(2,1)S(1)} %get-tuple-element.19.chosen, f32[328,512]{1,0:T(8,128)S(1)} %get-tuple-element.20.refs_0_, ...), custom_call_target="tpu_custom_call", output_to_operand_aliasing={{0}: (8, {}), {1}: (9, {}), {2}: (10, {})} | custom-call | flops 6000000000 | tf_op jit(solution)/shard_map/correct_and_pack/pallas_call | solution.py:780
  46.3 29.8 %all_to_all.5.got = f32[128,1,2176]{2,1,0:T(1,128)S(1)} all-to-all(f32[128,1,2176]{2,1,0:T(1,128)S(1)} %get-tuple-element.26), channel_id=1, replica_groups=mesh['gx'=8,'gy'=16] {'gx','gy'}, dimensions={0} | all-to-all | bytes 2228224 | tf_op jit(solution)/shard_map/all_to_all | solution.py:845
  76.1 2.4 %place_rows.1 = f32[64,2048]{1,0:T(8,128)} custom-call(f32[128,1,2176]{2,1,0:T(1,128)S(1)} %all_to_all.5.got), custom_call_target="tpu_custom_call" | custom-call | flops 2000000000 | tf_op jit(solution)/shard_map/place_rows/pallas_call | solution.py:822
  (4 shorter events, 0.0 us)
Async XLA Ops:
  5.6 16.4 %collective-permute-start.1 = (f32[10,16,512]{2,1,0:T(8,128)}, f32[10,16,512]{2,1,0:T(8,128)S(1)}, u32[]{:S(2)}, u32[]{:S(2)}) collective-permute-start(f32[10,16,512]{2,1,0:T(8,128)} %get-tuple-element.17), channel_id=1, source_target_pairs={{0,15},{1,0},{2,1},{3,2},{4,3},{5,4},{6,5},{7,6},{8,7},{9,8},{10,9... | collective-permute-start | bytes 983048 | tf_op jit(solution)/shard_map/ppermute | solution.py:27
  7.1 14.9 %collective-permute-start = (f32[14,16,512]{2,1,0:T(8,128)}, f32[14,16,512]{2,1,0:T(8,128)S(1)}, u32[]{:S(2)}, u32[]{:S(2)}) collective-permute-start(f32[14,16,512]{2,1,0:T(8,128)} %get-tuple-element.16), channel_id=1, source_target_pairs={{0,1},{1,2},{2,3},{3,4},{4,5},{5,6},{6,7},{7,8},{8,9},{9,10},{10,1... | collective-permute-start | bytes 1376264 | tf_op jit(solution)/shard_map/ppermute | solution.py:27
  10.8 1.9 %copy-start = (f32[3,16,32,512]{3,2,1,0:T(8,128)S(1)}, f32[3,16,32,512]{3,2,1,0:T(8,128)}, u32[]{:S(2)}) copy-start(f32[3,16,32,512]{3,2,1,0:T(8,128)} %refs_0_.3) | copy-start | bytes 9437188
  12.7 1.9 %copy-start.1 = (f32[3,16,32,512]{3,2,1,0:T(8,128)S(1)}, f32[3,16,32,512]{3,2,1,0:T(8,128)}, u32[]{:S(2)}) copy-start(f32[3,16,32,512]{3,2,1,0:T(8,128)} %refs_1_.3) | copy-start | bytes 9437188
  14.6 1.9 %copy-start.2 = (f32[3,16,32,512]{3,2,1,0:T(8,128)S(1)}, f32[3,16,32,512]{3,2,1,0:T(8,128)}, u32[]{:S(2)}) copy-start(f32[3,16,32,512]{3,2,1,0:T(8,128)} %refs_2_.3) | copy-start | bytes 9437188
  16.5 1.9 %copy-start.3 = (f32[3,16,32,512]{3,2,1,0:T(8,128)S(1)}, f32[3,16,32,512]{3,2,1,0:T(8,128)}, u32[]{:S(2)}) copy-start(f32[3,16,32,512]{3,2,1,0:T(8,128)} %refs_3_.3) | copy-start | bytes 9437188
  18.3 1.2 %copy-start.4 = (f32[16,32,512]{2,1,0:T(8,128)S(1)}, f32[16,32,512]{2,1,0:T(8,128)}, u32[]{:S(2)}) copy-start(f32[16,32,512]{2,1,0:T(8,128)} %refs_5_.4) | copy-start | bytes 3145732
  19.6 1.2 %copy-start.5 = (f32[16,32,512]{2,1,0:T(8,128)S(1)}, f32[16,32,512]{2,1,0:T(8,128)}, u32[]{:S(2)}) copy-start(f32[16,32,512]{2,1,0:T(8,128)} %refs_6_.3) | copy-start | bytes 3145732
  20.8 1.2 %copy-start.6 = (f32[16,32,512]{2,1,0:T(8,128)S(1)}, f32[16,32,512]{2,1,0:T(8,128)}, u32[]{:S(2)}) copy-start(f32[16,32,512]{2,1,0:T(8,128)} %refs_5_.5) | copy-start | bytes 3145732
  22.9 17.4 %collective-permute-start.3 = (f32[328,512]{1,0:T(8,128)S(1)}, f32[328,512]{1,0:T(8,128)S(1)}, u32[]{:S(2)}, u32[]{:S(2)}) collective-permute-start(f32[328,512]{1,0:T(8,128)S(1)} %get-tuple-element.20.refs_0_), channel_id=1, source_target_pairs={{0,112},{16,0},{32,16},{48,32},{64,48},{80,64},{96,80},{112,96},{1... | collective-permute-start | bytes 2015240 | tf_op jit(solution)/shard_map/ppermute | solution.py:27
  25.9 13.3 %copy-start.8 = (s32[1,1,128]{2,1,0:T(1,128)S(1)}, s32[1,1,128]{2,1,0:T(1,128)}, u32[]{:S(2)}) copy-start(s32[1,1,128]{2,1,0:T(1,128)} %mask.1) | copy-start | bytes 1540
  25.9 13.3 %copy-start.9 = (s32[1,1,128]{2,1,0:T(1,128)S(1)}, s32[1,1,128]{2,1,0:T(1,128)}, u32[]{:S(2)}) copy-start(s32[1,1,128]{2,1,0:T(1,128)} %param.21) | copy-start | bytes 1540
  25.9 15.7 %collective-permute-start.2 = (f32[328,512]{1,0:T(8,128)S(1)}, f32[328,512]{1,0:T(8,128)S(1)}, u32[]{:S(2)}, u32[]{:S(2)}) collective-permute-start(f32[328,512]{1,0:T(8,128)S(1)} %get-tuple-element.22.refs_2_), channel_id=1, source_target_pairs={{0,16},{16,32},{32,48},{48,64},{64,80},{80,96},{96,112},{112,0},{1... | collective-permute-start | bytes 2015240 | tf_op jit(solution)/shard_map/ppermute | solution.py:27
  39.2 2.4 %copy-start.7 = (f32[16,32,512]{2,1,0:T(8,128)S(1)}, f32[16,32,512]{2,1,0:T(8,128)}, u32[]{:S(2)}) copy-start(f32[16,32,512]{2,1,0:T(8,128)} %refs_5_.5) | copy-start | bytes 3145732
